TPU v7x, 32 devices: a whole 2x2x4 slice. The times are simulated.
32 devices in a mesh: comp: 2 (over core), lat: 8 (over z, y), lon: 2 (over x).
Axes of the slice: x: 2, y: 2, z: 4, core: 2. Of those that a mesh axis runs over, the one named last changes fastest.
Arguments:
- innovations: float32 [2, 3, 2048, 512], P('comp', None, ('lat', 'lon')), may hold values from -6 to 6
- obs_owner: int32 [2, 3, 2048, 1], P('comp', None, ('lat', 'lon')), may hold values from 0 to 15; in each aligned block of 128 rows (0 to 127, 128 to 255, ..., all dimensions but the last counted through in order) at most 16 rows name the same one
- obs_cell: int32 [2, 3, 2048], P('comp', None, ('lat', 'lon')), may hold values from 0 to 1023
- velocity: float32 [2, 3, 2, 128, 64, 256], P('comp', None, None, None, 'lat', 'lon'), may hold values from -0.2 to 0.2
- diffusion: float32 [2, 3, 2, 128, 64, 256], P('comp', None, None, None, 'lat', 'lon'), may hold values from 0.01 to 0.08
- mixing: float32 [2, 4, 4], P('comp'), may hold values from -0.15 to 0.15
- air_sea: float32 [4, 4], replicated, may hold values from -1 to 1
- sea_mask: int32 [64, 256], P('lat', 'lon'), may hold values 0 or 1
Outputs:
- gradient: float32 [2, 4, 128, 64, 256], P('comp', None, None, 'lat', 'lon')
Inputs may be any that keep to these rules, and one draw needn't show every extreme that they name: `obs_owner`: among the 128 rows of one device for one section and timestep, no owner is named more than 16 times, a bound that some block reaches.
All inputs are finite; a program needn't handle non-finite values. No bound on the sum of `sea_mask` on one device may be relied on, other than what follows from the above.
Results may differ from a plain program's by a relative error of at most 0.0001.
Values sent between devices are 32-bit elements; how exact they have to be, the bound alone decides.
A program may use at most 320 MiB of HBM per device.

v0:
```python
import functools

import jax
import jax.numpy as jnp
from jax import lax
from jax.experimental import pallas as pl
from jax.experimental.pallas import tpu as pltpu
from jax.sharding import PartitionSpec as P

MESH = pl.DeviceIdType.MESH
LANES = 128
SUB = 8


def split3(x):
    hi = x.astype(jnp.bfloat16)
    rest = x - hi.astype(jnp.float32)
    mid = rest.astype(jnp.bfloat16)
    lo = (rest - mid.astype(jnp.float32)).astype(jnp.bfloat16)
    return hi, mid, lo


def sweep(
    dims,
    innov,
    owner_ref,
    cell_ref,
    vel,
    dif,
    mix_ref,
    air_ref,
    sea_ref,
    out_ref,
    inn_v,
    vel_v,
    dif_v,
    send,
    recv,
    cells_s,
    cells_r,
    rimn_s,
    rimn_r,
    rime_s,
    rime_r,
    state,
    halo,
    side_s,
    side_r,
    top_s,
    top_r,
    spread,
    place,
    load_sem,
    data_ss,
    data_rs,
    cell_ss,
    cell_rs,
    rim_ss,
    rim_rs,
    halo_ss,
    halo_rs,
    side_ss,
    side_rs,
    top_ss,
    top_rs,
):
    steps, fields, levels, rows, obs, lat_n, lon_n, cap = dims
    n = lat_n * lon_n
    slots = n * cap
    tiles = slots // LANES
    per_tile = LANES // cap
    fl = fields * levels
    blocks = levels // SUB
    comp = lax.axis_index("comp")
    lat = lax.axis_index("lat")
    lon = lax.axis_index("lon")
    me = lat * lon_n + lon
    east = lax.rem(lon + 1, lon_n)
    west = lax.rem(lon + lon_n - 1, lon_n)
    is_ocean = comp == 1
    order = list(reversed(range(steps)))

    def at_offset(k):
        peer = lax.rem(me + k, n)
        return (comp, peer // lon_n, lax.rem(peer, lon_n))

    loads = {}
    for t in order:
        loads["i", t] = pltpu.make_async_copy(innov.at[t], inn_v.at[t], load_sem.at[0, t])
        loads["i", t].start()
    for t in order:
        loads["v", t] = pltpu.make_async_copy(vel.at[t], vel_v.at[t], load_sem.at[1, t])
        loads["d", t] = pltpu.make_async_copy(dif.at[t], dif_v.at[t], load_sem.at[2, t])
        loads["v", t].start()
        loads["d", t].start()

    barrier = pltpu.get_barrier_semaphore()

    @pl.loop(1, n)
    def _(k):
        pl.semaphore_signal(barrier, inc=1, device_id=at_offset(k), device_id_type=MESH)

    pl.semaphore_signal(barrier, inc=1, device_id=(1 - comp, lat, lon), device_id_type=MESH)

    sub_i = lax.broadcasted_iota(jnp.int32, (obs, obs), 0)
    lane_i = lax.broadcasted_iota(jnp.int32, (obs, obs), 1)
    earlier = sub_i < lane_i
    lane1 = lax.broadcasted_iota(jnp.int32, (1, LANES), 1)
    lane8 = lax.broadcasted_iota(jnp.int32, (SUB, LANES), 1)

    def picks(t):
        owner = owner_ref[t : t + 1, :]
        across = jnp.broadcast_to(owner.astype(jnp.float32), (obs, obs))
        down = across.T
        rank = jnp.sum(
            jnp.where((across == down) & earlier, 1.0, 0.0), axis=0, keepdims=True
        ).astype(jnp.int32)
        shift = owner - me
        offset = jnp.where(shift < 0, shift + n, shift)
        target = offset * cap + rank
        slot_i = lax.broadcasted_iota(jnp.int32, (slots, obs), 0)
        return jnp.where(slot_i == target, 1.0, 0.0)

    for t in order:
        hot = picks(t)
        cells = jnp.broadcast_to(cell_ref[t : t + 1, :].astype(jnp.float32) + 1.0, (SUB, obs))
        at = (
            lax.dot_general(
                cells,
                hot,
                (((1,), (1,)), ((), ())),
                precision=lax.Precision.HIGHEST,
                preferred_element_type=jnp.float32,
            )
            - 1.0
        )
        for i in range(tiles):
            cells_s[i, t : t + 1, :] = at[0:1, i * LANES : (i + 1) * LANES]

    pl.semaphore_wait(barrier, n)

    def cell_copy(k):
        return pltpu.make_async_remote_copy(
            src_ref=cells_s.at[k // per_tile],
            dst_ref=cells_r.at[k],
            send_sem=cell_ss.at[k],
            recv_sem=cell_rs.at[k],
            device_id=at_offset(k),
            device_id_type=MESH,
        )

    def data_copy(t, k):
        return pltpu.make_async_remote_copy(
            src_ref=send.at[t, k],
            dst_ref=recv.at[t, k],
            send_sem=data_ss.at[t, k],
            recv_sem=data_rs.at[t, k],
            device_id=at_offset(k),
            device_id_type=MESH,
        )

    def north_rim_copy():
        return pltpu.make_async_remote_copy(
            src_ref=rimn_s,
            dst_ref=rimn_r,
            send_sem=rim_ss.at[0],
            recv_sem=rim_rs.at[0],
            device_id=(comp, lax.rem(lat + 1, lat_n), lon),
            device_id_type=MESH,
        )

    def east_rim_copy():
        return pltpu.make_async_remote_copy(
            src_ref=rime_s,
            dst_ref=rime_r,
            send_sem=rim_ss.at[1],
            recv_sem=rim_rs.at[1],
            device_id=(comp, lat, east),
            device_id_type=MESH,
        )

    def halo_copy(t, up):
        return pltpu.make_async_remote_copy(
            src_ref=state.at[t, rows - 1 if up else 0],
            dst_ref=halo.at[t, 0 if up else 1],
            send_sem=halo_ss.at[t, 0 if up else 1],
            recv_sem=halo_rs.at[t, 0 if up else 1],
            device_id=(comp, lax.rem(lat + (1 if up else lat_n - 1), lat_n), lon),
            device_id_type=MESH,
        )

    def side_copy(t, to_east):
        return pltpu.make_async_remote_copy(
            src_ref=side_s.at[t],
            dst_ref=side_r.at[t, 1 if to_east else 0],
            send_sem=side_ss.at[t, 1 if to_east else 0],
            recv_sem=side_rs.at[t, 1 if to_east else 0],
            device_id=(comp, lat, east if to_east else west),
            device_id_type=MESH,
        )

    def top_copy(t):
        return pltpu.make_async_remote_copy(
            src_ref=top_s.at[t],
            dst_ref=top_r.at[t],
            send_sem=top_ss.at[t],
            recv_sem=top_rs.at[t],
            device_id=(1 - comp, lat, lon),
            device_id_type=MESH,
        )

    sides = (True,) if lon_n == 2 else (True, False)
    not_last = lat < lat_n - 1
    not_first = lat > 0

    @pl.loop(1, n)
    def _(k):
        cell_copy(k).start()

    for i in range(1):
        cells_r[0] = cells_s[0]

    def pack(t):
        loads["i", t].wait()
        hot = picks(t).astype(jnp.bfloat16)
        hi, mid, lo = split3(inn_v[t])
        packed = jnp.dot(
            jnp.concatenate([hot, hot, hot], axis=1),
            jnp.concatenate([hi, mid, lo], axis=0),
            preferred_element_type=jnp.float32,
        ).reshape(n, cap, fl)
        send[t] = packed
        recv[t, 0] = packed[0]

    def ship(t):
        @pl.loop(1, n)
        def _(k):
            data_copy(t, k).start()

    pack(order[0])
    ship(order[0])

    for t in order:
        loads["v", t].wait()
        loads["d", t].wait()

        @pl.loop(0, blocks)
        def _(b):
            edge = pl.ds(b * (SUB * rows) + rows - 1, SUB, stride=rows)
            fall = jnp.minimum(vel_v[t, 1, edge, :], 0.0) - dif_v[t, 1, edge, :]
            rimn_s[t, pl.ds(pl.multiple_of(b * SUB, SUB), SUB), :] = fall
            packed = rime_s[t]
            for y in range(rows):
                line = pl.ds(b * (SUB * rows) + y, SUB, stride=rows)
                fall = jnp.minimum(vel_v[t, 0, line, :], 0.0) - dif_v[t, 0, line, :]
                q = b * rows + y
                packed = jnp.where(lane8 == q, pltpu.roll(fall, lax.rem(q + 1, LANES), 1), packed)
            rime_s[t] = packed

    @pl.when(not_last)
    def _():
        north_rim_copy().start()

    east_rim_copy().start()

    @pl.when(jnp.logical_not(not_first))
    def _():
        rimn_r[...] = jnp.zeros_like(rimn_r)
        for t in order:
            halo[t, 0] = jnp.zeros((fl, LANES), jnp.float32)

    @pl.when(jnp.logical_not(not_last))
    def _():
        for t in order:
            halo[t, 1] = jnp.zeros((fl, LANES), jnp.float32)

    for t in order[1:]:
        pack(t)
    if steps > 1:
        ship(order[1])

    @pl.loop(1, n)
    def _(k):
        cell_copy(k).wait_recv()

    land = [
        jnp.where(is_ocean, sea_ref[y : y + 1, :].astype(jnp.float32), 1.0) for y in range(rows)
    ]
    open_last = jnp.where(not_last, 1.0, 0.0)

    for turn, t in enumerate(order):
        first = turn == 0

        @pl.loop(1, n)
        def _(k):
            data_copy(t, k).wait_recv()

        for i in range(tiles):
            line = jnp.full((1, LANES), -1.0, jnp.float32)
            for j in range(per_tile):
                k = i * per_tile + j
                line = jnp.where(lane1 // cap == j, cells_r[k, t : t + 1, :], line)
            place[i * LANES : (i + 1) * LANES, :] = jnp.broadcast_to(line, (LANES, LANES)).T

        for i in range(tiles):
            part = recv[t, i * per_tile : (i + 1) * per_tile].reshape(LANES, fl)
            hi, mid, lo = split3(part.T)
            spread[:, i * LANES : (i + 1) * LANES] = hi
            spread[:, slots + i * LANES : slots + (i + 1) * LANES] = mid
            spread[:, 2 * slots + i * LANES : 2 * slots + (i + 1) * LANES] = lo

        def add_forcing(y):
            lane_s = lax.broadcasted_iota(jnp.int32, (slots, LANES), 1)
            col = lane_s.astype(jnp.float32)
            where_to = place[...]
            hot = jnp.concatenate(
                [
                    jnp.where(where_to == col + float(v * LANES), 1.0, 0.0).astype(jnp.bfloat16)
                    for v in (y, y + 1)
                ],
                axis=1,
            )
            hot3 = jnp.concatenate([hot, hot, hot], axis=0)
            for f in range(fields):
                part = slice(f * levels, (f + 1) * levels)
                got = jnp.dot(spread[part, :], hot3, preferred_element_type=jnp.float32)
                for v in (0, 1):
                    new = got[:, v * LANES : (v + 1) * LANES]
                    if not first:
                        new = new + state[t, y + v, part, :]
                    state[t, y + v, part, :] = new * land[y + v]

        add_forcing(0)

        @pl.when(not_first)
        def _():
            halo_copy(t, False).start()

        add_forcing(rows - 2)

        @pl.when(not_last)
        def _():
            halo_copy(t, True).start()

        for y in range(2, rows - 2, 2):
            add_forcing(y)

        @pl.loop(0, blocks)
        def _(b):
            half = b // SUB
            dst = pl.ds(pl.multiple_of(lax.rem(b, SUB) * SUB, SUB), SUB)
            packed = side_s[t, dst, :]
            for y in range(rows):
                for f in range(fields):
                    q = half * (rows * fields) + y * fields + f
                    src = pl.ds(pl.multiple_of(f * levels + b * SUB, SUB), SUB)
                    turned = pltpu.roll(state[t, y, src, :], 2 * q + 1, 1)
                    packed = jnp.where(lane8 // 2 == q, turned, packed)
            side_s[t, dst, :] = packed

        for to_east in sides:
            side_copy(t, to_east).start()

        @pl.when(jnp.logical_not(is_ocean))
        def _():
            for f in range(fields):
                for y in range(rows):
                    at = f * levels + levels - 1
                    top_s[t, f * rows + y : f * rows + y + 1, :] = state[t, y, at : at + 1, :]
            top_copy(t).start()

        if turn + 2 < steps:
            ship(order[turn + 2])

        if first:

            @pl.when(not_first)
            def _():
                north_rim_copy().wait_recv()

            east_rim_copy().wait_recv()

        for to_east in sides:
            side_copy(t, to_east).wait_recv()

        @pl.when(not_first)
        def _():
            halo_copy(t, True).wait_recv()

        @pl.when(not_last)
        def _():
            halo_copy(t, False).wait_recv()

        last = turn == steps - 1

        @pl.loop(0, blocks)
        def _(b):
            half = b // SUB
            lev = pl.ds(pl.multiple_of(b * SUB, SUB), SUB)
            fls = [pl.ds(pl.multiple_of(f * levels + b * SUB, SUB), SUB) for f in range(fields)]
            lo = pl.ds(pl.multiple_of(lax.rem(b, SUB) * SUB, SUB), SUB)
            if lon_n == 2:
                edge = side_r[t, 1, lo, :]
            else:
                edge = jnp.where(lax.rem(lane8, 2) == 1, side_r[t, 0, lo, :], side_r[t, 1, lo, :])
            rim_e = rime_r[t]
            below = [halo[t, 0, s, :] for s in fls]
            here = [state[t, 0, s, :] for s in fls]
            fall_n = rimn_r[t, lev, :]
            for y in range(rows):
                if y < rows - 1:
                    above = [state[t, y + 1, s, :] for s in fls]
                else:
                    above = [halo[t, 1, s, :] for s in fls]
                line = pl.ds(b * (SUB * rows) + y, SUB, stride=rows)
                we, ke = vel_v[t, 0, line, :], dif_v[t, 0, line, :]
                wn, kn = vel_v[t, 1, line, :], dif_v[t, 1, line, :]
                up_e = jnp.maximum(we, 0.0) + ke
                fall_e = pltpu.roll(jnp.minimum(we, 0.0) - ke, 1, 1)
                from_west = pltpu.roll(rim_e, lax.rem(LANES - (b * rows + y), LANES), 1)
                fall_e = jnp.where(lane8 == 0, from_west, fall_e)
                up_n = jnp.maximum(wn, 0.0) + kn
                next_fall = jnp.minimum(wn, 0.0) - kn
                if y == rows - 1:
                    up_n = up_n * open_last
                for g in range(fields):
                    m = here[g]
                    q = half * (rows * fields) + y * fields + g
                    rim = pltpu.roll(edge, LANES - 1 - 2 * q, 1)
                    m_east = pltpu.roll(jnp.where(lane8 == 0, rim, m), LANES - 1, 1)
                    m_west = pltpu.roll(jnp.where(lane8 == LANES - 1, rim, m), 1, 1)
                    res = m
                    for f in range(fields):
                        res = res + mix_ref[f, g] * here[f]
                    res = res + up_e * (m_east - m) + fall_e * (m - m_west)
                    res = res + up_n * (above[g] - m) + fall_n * (m - below[g])
                    if last:
                        spot = pl.ds(
                            g * (levels * rows) + b * (SUB * rows) + y, SUB, stride=rows
                        )
                        out_ref[spot, :] = res
                    else:
                        state[order[turn + 1] if not last else 0, y, fls[g], :] = res
                below, here, fall_n = here, above, next_fall

        @pl.when(is_ocean)
        def _():
            top_copy(t).wait_recv()
            for g in range(fields):
                flux = air_ref[0, g] * top_r[t, 0:rows, :]
                for f in range(1, fields):
                    flux = flux + air_ref[f, g] * top_r[t, f * rows : (f + 1) * rows, :]
                flux = flux * sea_ref[...].astype(jnp.float32)
                if last:
                    spot = slice(g * levels * rows, g * levels * rows + rows)
                    out_ref[spot, :] = out_ref[spot, :] + flux
                else:
                    nxt = order[turn + 1]
                    at = g * levels
                    for y in range(rows):
                        state[nxt, y, at : at + 1, :] = (
                            state[nxt, y, at : at + 1, :] + flux[y : y + 1, :]
                        )

    @pl.loop(1, n)
    def _(k):
        cell_copy(k).wait_send()
        for t in order:
            data_copy(t, k).wait_send()

    east_rim_copy().wait_send()

    @pl.when(not_last)
    def _():
        north_rim_copy().wait_send()

    for t in order:
        for to_east in sides:
            side_copy(t, to_east).wait_send()

        @pl.when(not_first)
        def _():
            halo_copy(t, False).wait_send()

        @pl.when(not_last)
        def _():
            halo_copy(t, True).wait_send()

        @pl.when(jnp.logical_not(is_ocean))
        def _():
            top_copy(t).wait_send()


def shards(lat_n, lon_n, innovations, obs_owner, obs_cell, velocity, diffusion, mixing, air_sea, sea_mask):
    steps, levels, rows, cols = (velocity.shape[i] for i in (1, 3, 4, 5))
    fields = mixing.shape[1]
    obs = innovations.shape[2]
    fl = fields * levels
    n = lat_n * lon_n
    cap = max(SUB, 2 * obs // n)
    slots = n * cap
    tiles = slots // LANES
    dims = (steps, fields, levels, rows, obs, lat_n, lon_n, cap)
    vmem = pl.BlockSpec(memory_space=pltpu.VMEM)
    smem = pl.BlockSpec(memory_space=pltpu.SMEM)
    hbm = pl.BlockSpec(memory_space=pl.ANY)
    f32 = jnp.float32
    dma = pltpu.SemaphoreType.DMA
    out = pl.pallas_call(
        functools.partial(sweep, dims),
        out_shape=jax.ShapeDtypeStruct((fl * rows, cols), f32),
        in_specs=[hbm, vmem, vmem, hbm, hbm, smem, smem, vmem],
        out_specs=vmem,
        scratch_shapes=[
            pltpu.VMEM((steps, obs, fl), f32),
            pltpu.VMEM((steps, 2, levels * rows, cols), f32),
            pltpu.VMEM((steps, 2, levels * rows, cols), f32),
            pltpu.VMEM((steps, n, cap, fl), f32),
            pltpu.VMEM((steps, n, cap, fl), f32),
            pltpu.VMEM((tiles, SUB, LANES), f32),
            pltpu.VMEM((n, SUB, LANES), f32),
            pltpu.VMEM((steps, levels, cols), f32),
            pltpu.VMEM((steps, levels, cols), f32),
            pltpu.VMEM((steps, SUB, cols), f32),
            pltpu.VMEM((steps, SUB, cols), f32),
            pltpu.VMEM((steps, rows, fl, cols), f32),
            pltpu.VMEM((steps, 2, fl, cols), f32),
            pltpu.VMEM((steps, SUB * SUB, cols), f32),
            pltpu.VMEM((steps, 2, SUB * SUB, cols), f32),
            pltpu.VMEM((steps, fields * rows, cols), f32),
            pltpu.VMEM((steps, fields * rows, cols), f32),
            pltpu.VMEM((fl, 3 * slots), jnp.bfloat16),
            pltpu.VMEM((slots, LANES), f32),
            dma((3, steps)),
            dma((steps, n)),
            dma((steps, n)),
            dma((n,)),
            dma((n,)),
            dma((2,)),
            dma((2,)),
            dma((steps, 2)),
            dma((steps, 2)),
            dma((steps, 2)),
            dma((steps, 2)),
            dma((steps,)),
            dma((steps,)),
        ],
        compiler_params=pltpu.CompilerParams(
            collective_id=0, has_side_effects=True, vmem_limit_bytes=56 * 1024 * 1024
        ),
    )(
        innovations[0],
        obs_owner[0, :, :, 0],
        obs_cell[0],
        velocity[0].reshape(steps, 2, levels * rows, cols),
        diffusion[0].reshape(steps, 2, levels * rows, cols),
        mixing[0],
        air_sea,
        sea_mask,
    )
    return out.reshape(1, fields, levels, rows, cols)


def solution(mesh):
    return jax.shard_map(
        functools.partial(shards, mesh.shape["lat"], mesh.shape["lon"]),
        mesh=mesh,
        in_specs=(
            P("comp", None, ("lat", "lon"), None),
            P("comp", None, ("lat", "lon"), None),
            P("comp", None, ("lat", "lon")),
            P("comp", None, None, None, "lat", "lon"),
            P("comp", None, None, None, "lat", "lon"),
            P("comp", None, None),
            P(),
            P("lat", "lon"),
        ),
        out_specs=P("comp", None, None, "lat", "lon"),
        check_vma=False,
    )
```

profile of v0, /device:TPU:12, one launch (start us, length us, event | category | flops | bytes accessed | tf_op | source)
XLA Modules:
  0.0 87.8 jit_solution(6706216221038110430)
XLA Ops:
  0.0 1.3 %copy.14 = s32[1,3,128,1]{2,1,3,0:T(4,128)} copy(s32[1,3,128,1]{2,3,1,0:T(1,128)} %param.9) | data formatting | bytes 3072
  1.3 1.3 %copy.13 = s32[1,3,128]{2,1,0:T(4,128)} copy(s32[1,3,128]{2,0,1:T(1,128)} %param.10) | data formatting | bytes 3072
  2.5 82.2 %shard_map.82 = f32[4096,128]{1,0:T(8,128)} custom-call(f32[3,128,512]{2,1,0:T(8,128)} %bitcast.14, s32[3,128]{1,0:T(4,128)} %bitcast.15, s32[3,128]{1,0:T(4,128)} %bitcast.16, f32[3,2,1024,128]{3,2,1,0:T(8,128)} %bitcast.12, f32[3,2,1024,128]{3,2,1,0:T(8,128)} %bitcast.13, f32[4,4]{1,0:T(4,128)} %bitcast.17, f32[4,4]{1,0:T(4,128)} %air_ref.1, s32[8,128]{1,0:T(8,128)} %sea_ref.1), custom_call_target="tpu_custom_call" | custom-call | tf_op jit(solution)/shard_map/pallas_call | solution.py:509
  84.8 3.0 %copy.16 = f32[1,4,128,8,128]{4,3,2,1,0:T(8,128)} copy(f32[1,4,128,8,128]{4,3,2,1,0:T(8,128)} %bitcast.11) | data formatting | bytes 4194304
where the time goes:
time: 88 us; the launch traced here: 87.8 us
  Pallas kernels  82.2 us (93%)
  local copies, waits for them, and re-layouts  5.58 us (6%)
    pallas_call x1, Pallas kernels, shards(): pl.pallas_call(functools.partial(sweep, dims), out_shape=jax.ShapeDtypeSt...  82.2 us
    unnamed x3, local copies, waits for them, and re-layouts  5.58 us

commit v1 on v0

--- a/solution.py
+++ b/solution.py
@@ -64,13 +64,16 @@
     top_ss,
     top_rs,
 ):
-    steps, fields, levels, rows, obs, lat_n, lon_n, cap = dims
+    steps, fields, levels, rows, obs, lat_n, lon_n, cap, chunks, lag, window = dims
     n = lat_n * lon_n
     slots = n * cap
     tiles = slots // LANES
     per_tile = LANES // cap
     fl = fields * levels
     blocks = levels // SUB
+    depth = levels // chunks
+    width = fields * depth
+    chunk_blocks = depth // SUB
     comp = lax.axis_index("comp")
     lat = lax.axis_index("lat")
     lon = lax.axis_index("lon")
@@ -79,6 +82,7 @@
     west = lax.rem(lon + lon_n - 1, lon_n)
     is_ocean = comp == 1
     order = list(reversed(range(steps)))
+    units = [(t, c) for t in order for c in range(chunks)]
 
     def at_offset(k):
         peer = lax.rem(me + k, n)
@@ -109,7 +113,7 @@
     lane8 = lax.broadcasted_iota(jnp.int32, (SUB, LANES), 1)
 
     def picks(t):
-        owner = owner_ref[t : t + 1, :]
+        owner = owner_ref[t]
         across = jnp.broadcast_to(owner.astype(jnp.float32), (obs, obs))
         down = across.T
         rank = jnp.sum(
@@ -123,7 +127,7 @@
 
     for t in order:
         hot = picks(t)
-        cells = jnp.broadcast_to(cell_ref[t : t + 1, :].astype(jnp.float32) + 1.0, (SUB, obs))
+        cells = jnp.broadcast_to(cell_ref[t].astype(jnp.float32) + 1.0, (SUB, obs))
         at = (
             lax.dot_general(
                 cells,
@@ -149,12 +153,12 @@
             device_id_type=MESH,
         )
 
-    def data_copy(t, k):
+    def data_copy(t, c, k):
         return pltpu.make_async_remote_copy(
-            src_ref=send.at[t, k],
-            dst_ref=recv.at[t, k],
-            send_sem=data_ss.at[t, k],
-            recv_sem=data_rs.at[t, k],
+            src_ref=send.at[t, c, k],
+            dst_ref=recv.at[t, c, k],
+            send_sem=data_ss.at[t * chunks + c, k],
+            recv_sem=data_rs.at[t * chunks + c, k],
             device_id=at_offset(k),
             device_id_type=MESH,
         )
@@ -179,22 +183,23 @@
             device_id_type=MESH,
         )
 
-    def halo_copy(t, up):
+    def halo_copy(t, c, up):
+        part = pl.ds(c * width, width)
         return pltpu.make_async_remote_copy(
-            src_ref=state.at[t, rows - 1 if up else 0],
-            dst_ref=halo.at[t, 0 if up else 1],
-            send_sem=halo_ss.at[t, 0 if up else 1],
-            recv_sem=halo_rs.at[t, 0 if up else 1],
+            src_ref=state.at[t, rows - 1 if up else 0, part],
+            dst_ref=halo.at[t, 0 if up else 1, part],
+            send_sem=halo_ss.at[t * chunks + c, 0 if up else 1],
+            recv_sem=halo_rs.at[t * chunks + c, 0 if up else 1],
             device_id=(comp, lax.rem(lat + (1 if up else lat_n - 1), lat_n), lon),
             device_id_type=MESH,
         )
 
-    def side_copy(t, to_east):
+    def side_copy(t, c, to_east):
         return pltpu.make_async_remote_copy(
-            src_ref=side_s.at[t],
-            dst_ref=side_r.at[t, 1 if to_east else 0],
-            send_sem=side_ss.at[t, 1 if to_east else 0],
-            recv_sem=side_rs.at[t, 1 if to_east else 0],
+            src_ref=side_s.at[t, c],
+            dst_ref=side_r.at[t, c, 1 if to_east else 0],
+            send_sem=side_ss.at[t * chunks + c, 1 if to_east else 0],
+            recv_sem=side_rs.at[t * chunks + c, 1 if to_east else 0],
             device_id=(comp, lat, east if to_east else west),
             device_id_type=MESH,
         )
@@ -217,28 +222,43 @@
     def _(k):
         cell_copy(k).start()
 
-    for i in range(1):
-        cells_r[0] = cells_s[0]
+    cells_r[0] = cells_s[0]
 
     def pack(t):
         loads["i", t].wait()
         hot = picks(t).astype(jnp.bfloat16)
-        hi, mid, lo = split3(inn_v[t])
+        wide = inn_v[t]
+        by_chunk = jnp.concatenate(
+            [
+                wide[:, f * levels + c * depth : f * levels + (c + 1) * depth]
+                for c in range(chunks)
+                for f in range(fields)
+            ],
+            axis=1,
+        )
+        hi, mid, lo = split3(by_chunk)
         packed = jnp.dot(
             jnp.concatenate([hot, hot, hot], axis=1),
             jnp.concatenate([hi, mid, lo], axis=0),
             preferred_element_type=jnp.float32,
-        ).reshape(n, cap, fl)
-        send[t] = packed
-        recv[t, 0] = packed[0]
-
-    def ship(t):
+        )
+        for c in range(chunks):
+            part = packed[:, c * width : (c + 1) * width].reshape(n, cap, width)
+            send[t, c] = part
+            recv[t, c, 0] = part[0]
+
+    def ship(t, c):
         @pl.loop(1, n)
         def _(k):
-            data_copy(t, k).start()
-
+            data_copy(t, c, k).start()
+
+    packed_to = 1
     pack(order[0])
-    ship(order[0])
+    for i in range(min(window, len(units))):
+        while order.index(units[i][0]) >= packed_to:
+            pack(order[packed_to])
+            packed_to += 1
+        ship(*units[i])
 
     for t in order:
         loads["v", t].wait()
@@ -274,10 +294,8 @@
         for t in order:
             halo[t, 1] = jnp.zeros((fl, LANES), jnp.float32)
 
-    for t in order[1:]:
+    for t in order[packed_to:]:
         pack(t)
-    if steps > 1:
-        ship(order[1])
 
     @pl.loop(1, n)
     def _(k):
@@ -288,30 +306,35 @@
     ]
     open_last = jnp.where(not_last, 1.0, 0.0)
 
-    for turn, t in enumerate(order):
-        first = turn == 0
+    def forced_unit(i):
+        t, c = units[i]
+        first = t == order[0]
+        base = c * width
 
         @pl.loop(1, n)
         def _(k):
-            data_copy(t, k).wait_recv()
-
-        for i in range(tiles):
-            line = jnp.full((1, LANES), -1.0, jnp.float32)
-            for j in range(per_tile):
-                k = i * per_tile + j
-                line = jnp.where(lane1 // cap == j, cells_r[k, t : t + 1, :], line)
-            place[i * LANES : (i + 1) * LANES, :] = jnp.broadcast_to(line, (LANES, LANES)).T
-
-        for i in range(tiles):
-            part = recv[t, i * per_tile : (i + 1) * per_tile].reshape(LANES, fl)
+            data_copy(t, c, k).wait_recv()
+
+        if i + window < len(units):
+            ship(*units[i + window])
+
+        if c == 0:
+            for j in range(tiles):
+                line = jnp.full((1, LANES), -1.0, jnp.float32)
+                for h in range(per_tile):
+                    k = j * per_tile + h
+                    line = jnp.where(lane1 // cap == h, cells_r[k, t : t + 1, :], line)
+                place[j * LANES : (j + 1) * LANES, :] = jnp.broadcast_to(line, (LANES, LANES)).T
+
+        for j in range(tiles):
+            part = recv[t, c, j * per_tile : (j + 1) * per_tile].reshape(LANES, width)
             hi, mid, lo = split3(part.T)
-            spread[:, i * LANES : (i + 1) * LANES] = hi
-            spread[:, slots + i * LANES : slots + (i + 1) * LANES] = mid
-            spread[:, 2 * slots + i * LANES : 2 * slots + (i + 1) * LANES] = lo
+            spread[:, j * LANES : (j + 1) * LANES] = hi
+            spread[:, slots + j * LANES : slots + (j + 1) * LANES] = mid
+            spread[:, 2 * slots + j * LANES : 2 * slots + (j + 1) * LANES] = lo
 
         def add_forcing(y):
-            lane_s = lax.broadcasted_iota(jnp.int32, (slots, LANES), 1)
-            col = lane_s.astype(jnp.float32)
+            col = lax.broadcasted_iota(jnp.int32, (slots, LANES), 1).astype(jnp.float32)
             where_to = place[...]
             hot = jnp.concatenate(
                 [
@@ -321,58 +344,65 @@
                 axis=1,
             )
             hot3 = jnp.concatenate([hot, hot, hot], axis=0)
-            for f in range(fields):
-                part = slice(f * levels, (f + 1) * levels)
-                got = jnp.dot(spread[part, :], hot3, preferred_element_type=jnp.float32)
-                for v in (0, 1):
-                    new = got[:, v * LANES : (v + 1) * LANES]
-                    if not first:
-                        new = new + state[t, y + v, part, :]
-                    state[t, y + v, part, :] = new * land[y + v]
+            part = slice(base, base + width)
+            got = jnp.dot(spread[...], hot3, preferred_element_type=jnp.float32)
+            for v in (0, 1):
+                new = got[:, v * LANES : (v + 1) * LANES]
+                if not first:
+                    new = new + state[t, y + v, part, :]
+                state[t, y + v, part, :] = new * land[y + v]
 
         add_forcing(0)
 
         @pl.when(not_first)
         def _():
-            halo_copy(t, False).start()
+            halo_copy(t, c, False).start()
 
         add_forcing(rows - 2)
 
         @pl.when(not_last)
         def _():
-            halo_copy(t, True).start()
+            halo_copy(t, c, True).start()
 
         for y in range(2, rows - 2, 2):
             add_forcing(y)
 
-        @pl.loop(0, blocks)
+        halves = chunk_blocks // 2
+
+        @pl.loop(0, halves)
         def _(b):
-            half = b // SUB
-            dst = pl.ds(pl.multiple_of(lax.rem(b, SUB) * SUB, SUB), SUB)
-            packed = side_s[t, dst, :]
-            for y in range(rows):
+            dst = pl.ds(pl.multiple_of(b * SUB, SUB), SUB)
+            packed = jnp.zeros((SUB, LANES), jnp.float32)
+            for half in (0, 1):
+                for y in range(rows):
+                    for f in range(fields):
+                        q = half * (rows * fields) + y * fields + f
+                        start = base + f * depth + (half * halves + b) * SUB
+                        src = pl.ds(pl.multiple_of(start, SUB), SUB)
+                        turned = pltpu.roll(state[t, y, src, :], (2 * q + 1) % LANES, 1)
+                        packed = jnp.where(lane8 // 2 == q, turned, packed)
+            side_s[t, c, dst, :] = packed
+
+        for to_east in sides:
+            side_copy(t, c, to_east).start()
+
+        if c == chunks - 1:
+
+            @pl.when(jnp.logical_not(is_ocean))
+            def _():
                 for f in range(fields):
-                    q = half * (rows * fields) + y * fields + f
-                    src = pl.ds(pl.multiple_of(f * levels + b * SUB, SUB), SUB)
-                    turned = pltpu.roll(state[t, y, src, :], 2 * q + 1, 1)
-                    packed = jnp.where(lane8 // 2 == q, turned, packed)
-            side_s[t, dst, :] = packed
-
-        for to_east in sides:
-            side_copy(t, to_east).start()
-
-        @pl.when(jnp.logical_not(is_ocean))
-        def _():
-            for f in range(fields):
-                for y in range(rows):
-                    at = f * levels + levels - 1
-                    top_s[t, f * rows + y : f * rows + y + 1, :] = state[t, y, at : at + 1, :]
-            top_copy(t).start()
-
-        if turn + 2 < steps:
-            ship(order[turn + 2])
-
-        if first:
+                    for y in range(rows):
+                        at = base + (f + 1) * depth - 1
+                        top_s[t, f * rows + y : f * rows + y + 1, :] = state[t, y, at : at + 1, :]
+                top_copy(t).start()
+
+    def stepped_unit(i):
+        t, c = units[i]
+        base = c * width
+        last = t == order[-1]
+        nxt = order[min(order.index(t) + 1, steps - 1)]
+
+        if i == 0:
 
             @pl.when(not_first)
             def _():
@@ -381,28 +411,33 @@
             east_rim_copy().wait_recv()
 
         for to_east in sides:
-            side_copy(t, to_east).wait_recv()
+            side_copy(t, c, to_east).wait_recv()
 
         @pl.when(not_first)
         def _():
-            halo_copy(t, True).wait_recv()
+            halo_copy(t, c, True).wait_recv()
 
         @pl.when(not_last)
         def _():
-            halo_copy(t, False).wait_recv()
-
-        last = turn == steps - 1
-
-        @pl.loop(0, blocks)
+            halo_copy(t, c, False).wait_recv()
+
+        halves = chunk_blocks // 2
+
+        @pl.loop(0, chunk_blocks)
         def _(b):
-            half = b // SUB
-            lev = pl.ds(pl.multiple_of(b * SUB, SUB), SUB)
-            fls = [pl.ds(pl.multiple_of(f * levels + b * SUB, SUB), SUB) for f in range(fields)]
-            lo = pl.ds(pl.multiple_of(lax.rem(b, SUB) * SUB, SUB), SUB)
+            half = b // halves
+            level_block = c * chunk_blocks + b
+            lev = pl.ds(pl.multiple_of(level_block * SUB, SUB), SUB)
+            fls = [
+                pl.ds(pl.multiple_of(base + f * depth + b * SUB, SUB), SUB) for f in range(fields)
+            ]
+            lo = pl.ds(pl.multiple_of(lax.rem(b, halves) * SUB, SUB), SUB)
             if lon_n == 2:
-                edge = side_r[t, 1, lo, :]
+                edge = side_r[t, c, 1, lo, :]
             else:
-                edge = jnp.where(lax.rem(lane8, 2) == 1, side_r[t, 0, lo, :], side_r[t, 1, lo, :])
+                edge = jnp.where(
+                    lax.rem(lane8, 2) == 1, side_r[t, c, 0, lo, :], side_r[t, c, 1, lo, :]
+                )
             rim_e = rime_r[t]
             below = [halo[t, 0, s, :] for s in fls]
             here = [state[t, 0, s, :] for s in fls]
@@ -412,12 +447,13 @@
                     above = [state[t, y + 1, s, :] for s in fls]
                 else:
                     above = [halo[t, 1, s, :] for s in fls]
-                line = pl.ds(b * (SUB * rows) + y, SUB, stride=rows)
+                line = pl.ds(level_block * (SUB * rows) + y, SUB, stride=rows)
                 we, ke = vel_v[t, 0, line, :], dif_v[t, 0, line, :]
                 wn, kn = vel_v[t, 1, line, :], dif_v[t, 1, line, :]
                 up_e = jnp.maximum(we, 0.0) + ke
                 fall_e = pltpu.roll(jnp.minimum(we, 0.0) - ke, 1, 1)
-                from_west = pltpu.roll(rim_e, lax.rem(LANES - (b * rows + y), LANES), 1)
+                q = level_block * rows + y
+                from_west = pltpu.roll(rim_e, lax.rem(LANES - q, LANES), 1)
                 fall_e = jnp.where(lane8 == 0, from_west, fall_e)
                 up_n = jnp.maximum(wn, 0.0) + kn
                 next_fall = jnp.minimum(wn, 0.0) - kn
@@ -435,13 +471,15 @@
                     res = res + up_e * (m_east - m) + fall_e * (m - m_west)
                     res = res + up_n * (above[g] - m) + fall_n * (m - below[g])
                     if last:
-                        spot = pl.ds(
-                            g * (levels * rows) + b * (SUB * rows) + y, SUB, stride=rows
-                        )
-                        out_ref[spot, :] = res
+                        start = g * (levels * rows) + level_block * (SUB * rows) + y
+                        out_ref[pl.ds(start, SUB, stride=rows), :] = res
                     else:
-                        state[order[turn + 1] if not last else 0, y, fls[g], :] = res
+                        state[nxt, y, fls[g], :] = res
                 below, here, fall_n = here, above, next_fall
+
+    def couple(t):
+        last = t == order[-1]
+        nxt = order[min(order.index(t) + 1, steps - 1)]
 
         @pl.when(is_ocean)
         def _():
@@ -455,18 +493,27 @@
                     spot = slice(g * levels * rows, g * levels * rows + rows)
                     out_ref[spot, :] = out_ref[spot, :] + flux
                 else:
-                    nxt = order[turn + 1]
-                    at = g * levels
+                    at = g * depth
                     for y in range(rows):
                         state[nxt, y, at : at + 1, :] = (
                             state[nxt, y, at : at + 1, :] + flux[y : y + 1, :]
                         )
 
+    for i in range(len(units) + lag):
+        if i < len(units):
+            t, c = units[i]
+            if c == 0 and i > 0:
+                couple(order[order.index(t) - 1])
+            forced_unit(i)
+        if i >= lag:
+            stepped_unit(i - lag)
+    couple(order[-1])
+
     @pl.loop(1, n)
     def _(k):
         cell_copy(k).wait_send()
-        for t in order:
-            data_copy(t, k).wait_send()
+        for t, c in units:
+            data_copy(t, c, k).wait_send()
 
     east_rim_copy().wait_send()
 
@@ -474,20 +521,21 @@
     def _():
         north_rim_copy().wait_send()
 
-    for t in order:
+    for t, c in units:
         for to_east in sides:
-            side_copy(t, to_east).wait_send()
+            side_copy(t, c, to_east).wait_send()
 
         @pl.when(not_first)
         def _():
-            halo_copy(t, False).wait_send()
+            halo_copy(t, c, False).wait_send()
 
         @pl.when(not_last)
         def _():
-            halo_copy(t, True).wait_send()
-
-        @pl.when(jnp.logical_not(is_ocean))
-        def _():
+            halo_copy(t, c, True).wait_send()
+
+    @pl.when(jnp.logical_not(is_ocean))
+    def _():
+        for t in order:
             top_copy(t).wait_send()
 
 
@@ -500,7 +548,9 @@
     cap = max(SUB, 2 * obs // n)
     slots = n * cap
     tiles = slots // LANES
-    dims = (steps, fields, levels, rows, obs, lat_n, lon_n, cap)
+    chunks, lag, window = 2, 1, 2
+    width = fl // chunks
+    dims = (steps, fields, levels, rows, obs, lat_n, lon_n, cap, chunks, lag, window)
     vmem = pl.BlockSpec(memory_space=pltpu.VMEM)
     smem = pl.BlockSpec(memory_space=pltpu.SMEM)
     hbm = pl.BlockSpec(memory_space=pl.ANY)
@@ -515,8 +565,8 @@
             pltpu.VMEM((steps, obs, fl), f32),
             pltpu.VMEM((steps, 2, levels * rows, cols), f32),
             pltpu.VMEM((steps, 2, levels * rows, cols), f32),
-            pltpu.VMEM((steps, n, cap, fl), f32),
-            pltpu.VMEM((steps, n, cap, fl), f32),
+            pltpu.VMEM((steps, chunks, n, cap, width), f32),
+            pltpu.VMEM((steps, chunks, n, cap, width), f32),
             pltpu.VMEM((tiles, SUB, LANES), f32),
             pltpu.VMEM((n, SUB, LANES), f32),
             pltpu.VMEM((steps, levels, cols), f32),
@@ -525,23 +575,23 @@
             pltpu.VMEM((steps, SUB, cols), f32),
             pltpu.VMEM((steps, rows, fl, cols), f32),
             pltpu.VMEM((steps, 2, fl, cols), f32),
-            pltpu.VMEM((steps, SUB * SUB, cols), f32),
-            pltpu.VMEM((steps, 2, SUB * SUB, cols), f32),
+            pltpu.VMEM((steps, chunks, SUB * SUB // chunks, cols), f32),
+            pltpu.VMEM((steps, chunks, 2, SUB * SUB // chunks, cols), f32),
             pltpu.VMEM((steps, fields * rows, cols), f32),
             pltpu.VMEM((steps, fields * rows, cols), f32),
-            pltpu.VMEM((fl, 3 * slots), jnp.bfloat16),
+            pltpu.VMEM((width, 3 * slots), jnp.bfloat16),
             pltpu.VMEM((slots, LANES), f32),
             dma((3, steps)),
-            dma((steps, n)),
-            dma((steps, n)),
+            dma((steps * chunks, n)),
+            dma((steps * chunks, n)),
             dma((n,)),
             dma((n,)),
             dma((2,)),
             dma((2,)),
-            dma((steps, 2)),
-            dma((steps, 2)),
-            dma((steps, 2)),
-            dma((steps, 2)),
+            dma((steps * chunks, 2)),
+            dma((steps * chunks, 2)),
+            dma((steps * chunks, 2)),
+            dma((steps * chunks, 2)),
             dma((steps,)),
             dma((steps,)),
         ],
@@ -550,8 +600,8 @@
         ),
     )(
         innovations[0],
-        obs_owner[0, :, :, 0],
-        obs_cell[0],
+        obs_owner.reshape(steps, 1, obs),
+        obs_cell.reshape(steps, 1, obs),
         velocity[0].reshape(steps, 2, levels * rows, cols),
         diffusion[0].reshape(steps, 2, levels * rows, cols),
         mixing[0],

time: 88 us -> 77.2 us (0.88)
  Pallas kernels: 82.2 us -> 73.8 us
  local copies, waits for them, and re-layouts: 5.58 us -> 3.05 us
    pallas_call x1, Pallas kernels: 82.2 us -> 73.8 us  [shards(): pl.pallas_call(functools.partial(sweep, dims), out_shape=jax.ShapeDtypeSt...]
    unnamed x3 -> x1, local copies, waits for them, and re-layouts: 5.58 us -> 3.05 us
where the time goes in v1:
time: 77.2 us; the launch traced here: 76.9 us
  Pallas kernels  73.8 us (96%)
  local copies, waits for them, and re-layouts  3.05 us (4%)
    pallas_call x1, Pallas kernels, shards(): pl.pallas_call(functools.partial(sweep, dims), out_shape=jax.ShapeDtypeSt...  73.8 us
    unnamed x1, local copies, waits for them, and re-layouts  3.05 us

profile of v1, /device:TPU:12, one launch (start us, length us, event | category | flops | bytes accessed | tf_op | source)
XLA Modules:
  0.0 76.9 jit_solution(9463446327838976364)
XLA Ops:
  0.0 73.8 %shard_map.82 = f32[4096,128]{1,0:T(8,128)} custom-call(f32[3,128,512]{2,1,0:T(8,128)} %bitcast.10, s32[3,1,128]{2,1,0:T(1,128)} %bitcast.12, s32[3,1,128]{2,1,0:T(1,128)} %bitcast.13, f32[3,2,1024,128]{3,2,1,0:T(8,128)} %bitcast.8, f32[3,2,1024,128]{3,2,1,0:T(8,128)} %bitcast.9, f32[4,4]{1,0:T(4,128)} %bitcast.11, f32[4,4]{1,0:T(4,128)} %air_ref.1, ...), custom_call_target="tpu_custom_call" | custom-call | tf_op jit(solution)/shard_map/pallas_call | solution.py:559
  73.9 3.0 %copy.10 = f32[1,4,128,8,128]{4,3,2,1,0:T(8,128)} copy(f32[1,4,128,8,128]{4,3,2,1,0:T(8,128)} %bitcast.7) | data formatting | bytes 4194304

commit v2 on v1

--- a/solution.py
+++ b/solution.py
@@ -12,12 +12,9 @@
 SUB = 8
 
 
-def split3(x):
+def split2(x):
     hi = x.astype(jnp.bfloat16)
-    rest = x - hi.astype(jnp.float32)
-    mid = rest.astype(jnp.bfloat16)
-    lo = (rest - mid.astype(jnp.float32)).astype(jnp.bfloat16)
-    return hi, mid, lo
+    return hi, (x - hi.astype(jnp.float32)).astype(jnp.bfloat16)
 
 
 def sweep(
@@ -50,6 +47,8 @@
     top_r,
     spread,
     place,
+    picked,
+    coef,
     load_sem,
     data_ss,
     data_rs,
@@ -86,7 +85,7 @@
 
     def at_offset(k):
         peer = lax.rem(me + k, n)
-        return (comp, peer // lon_n, lax.rem(peer, lon_n))
+        return (comp, lax.div(peer, lon_n), lax.rem(peer, lon_n))
 
     loads = {}
     for t in order:
@@ -125,19 +124,18 @@
         slot_i = lax.broadcasted_iota(jnp.int32, (slots, obs), 0)
         return jnp.where(slot_i == target, 1.0, 0.0)
 
-    for t in order:
-        hot = picks(t)
-        cells = jnp.broadcast_to(cell_ref[t].astype(jnp.float32) + 1.0, (SUB, obs))
-        at = (
-            lax.dot_general(
-                cells,
-                hot,
-                (((1,), (1,)), ((), ())),
-                precision=lax.Precision.HIGHEST,
-                preferred_element_type=jnp.float32,
-            )
-            - 1.0
-        )
+    def columns(t):
+        number = jnp.broadcast_to(cell_ref[t] + 1, (2 * SUB, obs))
+        row16 = lax.broadcasted_iota(jnp.int32, (2 * SUB, obs), 0)
+        coarse = lax.shift_right_logical(number, 5)
+        parts = jnp.where(row16 == 0, coarse * 32, jnp.where(row16 == 1, number - coarse * 32, 0))
+        at = lax.dot_general(
+            parts.astype(jnp.float32).astype(jnp.bfloat16),
+            picked[t],
+            (((1,), (1,)), ((), ())),
+            preferred_element_type=jnp.float32,
+        )
+        at = at[0:1, :] + at[1:2, :] - 1.0
         for i in range(tiles):
             cells_s[i, t : t + 1, :] = at[0:1, i * LANES : (i + 1) * LANES]
 
@@ -147,8 +145,8 @@
         return pltpu.make_async_remote_copy(
             src_ref=cells_s.at[k // per_tile],
             dst_ref=cells_r.at[k],
-            send_sem=cell_ss.at[k],
-            recv_sem=cell_rs.at[k],
+            send_sem=cell_ss.at[0],
+            recv_sem=cell_rs.at[0],
             device_id=at_offset(k),
             device_id_type=MESH,
         )
@@ -157,9 +155,30 @@
         return pltpu.make_async_remote_copy(
             src_ref=send.at[t, c, k],
             dst_ref=recv.at[t, c, k],
-            send_sem=data_ss.at[t * chunks + c, k],
-            recv_sem=data_rs.at[t * chunks + c, k],
+            send_sem=data_ss.at[t * chunks + c],
+            recv_sem=data_rs.at[t * chunks + c],
             device_id=at_offset(k),
+            device_id_type=MESH,
+        )
+
+    def data_all(t, c):
+        return pltpu.make_async_remote_copy(
+            src_ref=send.at[t, c, pl.ds(1, n - 1)],
+            dst_ref=recv.at[t, c, pl.ds(1, n - 1)],
+            send_sem=data_ss.at[t * chunks + c],
+            recv_sem=data_rs.at[t * chunks + c],
+            device_id=at_offset(1),
+            device_id_type=MESH,
+        )
+
+    def cells_all():
+        part = cells_r.at[pl.ds(1, n - 1)]
+        return pltpu.make_async_remote_copy(
+            src_ref=part,
+            dst_ref=part,
+            send_sem=cell_ss.at[0],
+            recv_sem=cell_rs.at[0],
+            device_id=at_offset(1),
             device_id_type=MESH,
         )
 
@@ -218,15 +237,10 @@
     not_last = lat < lat_n - 1
     not_first = lat > 0
 
-    @pl.loop(1, n)
-    def _(k):
-        cell_copy(k).start()
-
-    cells_r[0] = cells_s[0]
-
     def pack(t):
         loads["i", t].wait()
         hot = picks(t).astype(jnp.bfloat16)
+        picked[t] = hot
         wide = inn_v[t]
         by_chunk = jnp.concatenate(
             [
@@ -236,10 +250,9 @@
             ],
             axis=1,
         )
-        hi, mid, lo = split3(by_chunk)
         packed = jnp.dot(
-            jnp.concatenate([hot, hot, hot], axis=1),
-            jnp.concatenate([hi, mid, lo], axis=0),
+            jnp.concatenate([hot, hot], axis=1),
+            jnp.concatenate(split2(by_chunk), axis=0),
             preferred_element_type=jnp.float32,
         )
         for c in range(chunks):
@@ -252,12 +265,20 @@
         def _(k):
             data_copy(t, c, k).start()
 
-    packed_to = 1
     pack(order[0])
-    for i in range(min(window, len(units))):
-        while order.index(units[i][0]) >= packed_to:
-            pack(order[packed_to])
-            packed_to += 1
+    for i in range(min(window, chunks)):
+        ship(*units[i])
+    for t in order[1:]:
+        pack(t)
+    for t in order:
+        columns(t)
+
+    @pl.loop(1, n)
+    def _(k):
+        cell_copy(k).start()
+
+    cells_r[0] = cells_s[0]
+    for i in range(chunks, min(window, len(units))):
         ship(*units[i])
 
     for t in order:
@@ -266,15 +287,26 @@
 
         @pl.loop(0, blocks)
         def _(b):
-            edge = pl.ds(b * (SUB * rows) + rows - 1, SUB, stride=rows)
-            fall = jnp.minimum(vel_v[t, 1, edge, :], 0.0) - dif_v[t, 1, edge, :]
-            rimn_s[t, pl.ds(pl.multiple_of(b * SUB, SUB), SUB), :] = fall
             packed = rime_s[t]
+            lev = pl.ds(pl.multiple_of(b * SUB, SUB), SUB)
             for y in range(rows):
                 line = pl.ds(b * (SUB * rows) + y, SUB, stride=rows)
-                fall = jnp.minimum(vel_v[t, 0, line, :], 0.0) - dif_v[t, 0, line, :]
+                we, ke = vel_v[t, 0, line, :], dif_v[t, 0, line, :]
+                wn, kn = vel_v[t, 1, line, :], dif_v[t, 1, line, :]
+                fall_e = jnp.minimum(we, 0.0) - ke
                 q = b * rows + y
-                packed = jnp.where(lane8 == q, pltpu.roll(fall, lax.rem(q + 1, LANES), 1), packed)
+                packed = jnp.where(
+                    lane8 == q, pltpu.roll(fall_e, lax.rem(q + 1, LANES), 1), packed
+                )
+                up_n = jnp.maximum(wn, 0.0) + kn
+                fall_n = jnp.minimum(wn, 0.0) - kn
+                if y == rows - 1:
+                    up_n = up_n * jnp.where(not_last, 1.0, 0.0)
+                    rimn_s[t, lev, :] = fall_n
+                coef[t, 0, y, lev, :] = jnp.maximum(we, 0.0) + ke
+                coef[t, 1, y, lev, :] = pltpu.roll(fall_e, 1, 1)
+                coef[t, 2, y, lev, :] = up_n
+                coef[t, 3, y, lev, :] = fall_n
             rime_s[t] = packed
 
     @pl.when(not_last)
@@ -294,26 +326,18 @@
         for t in order:
             halo[t, 1] = jnp.zeros((fl, LANES), jnp.float32)
 
-    for t in order[packed_to:]:
-        pack(t)
-
-    @pl.loop(1, n)
-    def _(k):
-        cell_copy(k).wait_recv()
+    cells_all().wait_recv()
 
     land = [
         jnp.where(is_ocean, sea_ref[y : y + 1, :].astype(jnp.float32), 1.0) for y in range(rows)
     ]
-    open_last = jnp.where(not_last, 1.0, 0.0)
 
     def forced_unit(i):
         t, c = units[i]
         first = t == order[0]
         base = c * width
 
-        @pl.loop(1, n)
-        def _(k):
-            data_copy(t, c, k).wait_recv()
+        data_all(t, c).wait_recv()
 
         if i + window < len(units):
             ship(*units[i + window])
@@ -328,10 +352,9 @@
 
         for j in range(tiles):
             part = recv[t, c, j * per_tile : (j + 1) * per_tile].reshape(LANES, width)
-            hi, mid, lo = split3(part.T)
+            hi, rest = split2(part.T)
             spread[:, j * LANES : (j + 1) * LANES] = hi
-            spread[:, slots + j * LANES : slots + (j + 1) * LANES] = mid
-            spread[:, 2 * slots + j * LANES : 2 * slots + (j + 1) * LANES] = lo
+            spread[:, slots + j * LANES : slots + (j + 1) * LANES] = rest
 
         def add_forcing(y):
             col = lax.broadcasted_iota(jnp.int32, (slots, LANES), 1).astype(jnp.float32)
@@ -343,9 +366,9 @@
                 ],
                 axis=1,
             )
-            hot3 = jnp.concatenate([hot, hot, hot], axis=0)
+            hot2 = jnp.concatenate([hot, hot], axis=0)
             part = slice(base, base + width)
-            got = jnp.dot(spread[...], hot3, preferred_element_type=jnp.float32)
+            got = jnp.dot(spread[...], hot2, preferred_element_type=jnp.float32)
             for v in (0, 1):
                 new = got[:, v * LANES : (v + 1) * LANES]
                 if not first:
@@ -423,7 +446,7 @@
 
         halves = chunk_blocks // 2
 
-        @pl.loop(0, chunk_blocks)
+        @pl.loop(0, chunk_blocks, unroll=2)
         def _(b):
             half = b // halves
             level_block = c * chunk_blocks + b
@@ -438,6 +461,8 @@
                 edge = jnp.where(
                     lax.rem(lane8, 2) == 1, side_r[t, c, 0, lo, :], side_r[t, c, 1, lo, :]
                 )
+            even = lax.rem(lane8, 2) == 0
+            edge = jnp.where(even, pltpu.roll(edge, LANES - 1, 1), pltpu.roll(edge, 1, 1))
             rim_e = rime_r[t]
             below = [halo[t, 0, s, :] for s in fls]
             here = [state[t, 0, s, :] for s in fls]
@@ -447,24 +472,18 @@
                     above = [state[t, y + 1, s, :] for s in fls]
                 else:
                     above = [halo[t, 1, s, :] for s in fls]
-                line = pl.ds(level_block * (SUB * rows) + y, SUB, stride=rows)
-                we, ke = vel_v[t, 0, line, :], dif_v[t, 0, line, :]
-                wn, kn = vel_v[t, 1, line, :], dif_v[t, 1, line, :]
-                up_e = jnp.maximum(we, 0.0) + ke
-                fall_e = pltpu.roll(jnp.minimum(we, 0.0) - ke, 1, 1)
                 q = level_block * rows + y
                 from_west = pltpu.roll(rim_e, lax.rem(LANES - q, LANES), 1)
-                fall_e = jnp.where(lane8 == 0, from_west, fall_e)
-                up_n = jnp.maximum(wn, 0.0) + kn
-                next_fall = jnp.minimum(wn, 0.0) - kn
-                if y == rows - 1:
-                    up_n = up_n * open_last
+                up_e = coef[t, 0, y, lev, :]
+                fall_e = jnp.where(lane8 == 0, from_west, coef[t, 1, y, lev, :])
+                up_n = coef[t, 2, y, lev, :]
+                next_fall = coef[t, 3, y, lev, :]
                 for g in range(fields):
                     m = here[g]
                     q = half * (rows * fields) + y * fields + g
                     rim = pltpu.roll(edge, LANES - 1 - 2 * q, 1)
-                    m_east = pltpu.roll(jnp.where(lane8 == 0, rim, m), LANES - 1, 1)
-                    m_west = pltpu.roll(jnp.where(lane8 == LANES - 1, rim, m), 1, 1)
+                    m_east = jnp.where(lane8 == LANES - 1, rim, pltpu.roll(m, LANES - 1, 1))
+                    m_west = jnp.where(lane8 == 0, rim, pltpu.roll(m, 1, 1))
                     res = m
                     for f in range(fields):
                         res = res + mix_ref[f, g] * here[f]
@@ -509,11 +528,9 @@
             stepped_unit(i - lag)
     couple(order[-1])
 
-    @pl.loop(1, n)
-    def _(k):
-        cell_copy(k).wait_send()
-        for t, c in units:
-            data_copy(t, c, k).wait_send()
+    cells_all().wait_send()
+    for t, c in units:
+        data_all(t, c).wait_send()
 
     east_rim_copy().wait_send()
 
@@ -579,13 +596,15 @@
             pltpu.VMEM((steps, chunks, 2, SUB * SUB // chunks, cols), f32),
             pltpu.VMEM((steps, fields * rows, cols), f32),
             pltpu.VMEM((steps, fields * rows, cols), f32),
-            pltpu.VMEM((width, 3 * slots), jnp.bfloat16),
+            pltpu.VMEM((width, 2 * slots), jnp.bfloat16),
             pltpu.VMEM((slots, LANES), f32),
+            pltpu.VMEM((steps, slots, obs), jnp.bfloat16),
+            pltpu.VMEM((steps, 4, rows, levels, cols), f32),
             dma((3, steps)),
-            dma((steps * chunks, n)),
-            dma((steps * chunks, n)),
-            dma((n,)),
-            dma((n,)),
+            dma((steps * chunks,)),
+            dma((steps * chunks,)),
+            dma((1,)),
+            dma((1,)),
             dma((2,)),
             dma((2,)),
             dma((steps * chunks, 2)),

time: 77.2 us -> 75.5 us (0.978)
  the two profiles are of different devices: /device:TPU:12 before, /device:TPU:17 now
where the time goes in v2:
time: 75.5 us; the launch traced here: 75.3 us
  Pallas kernels  72.2 us (96%)
  local copies, waits for them, and re-layouts  3.05 us (4%)
    pallas_call x1, Pallas kernels, shards(): pl.pallas_call(functools.partial(sweep, dims), out_shape=jax.ShapeDtypeSt...  72.2 us
    unnamed x1, local copies, waits for them, and re-layouts  3.05 us

profile of v2, /device:TPU:17, one launch (start us, length us, event | category | flops | bytes accessed | tf_op | source)
XLA Modules:
  0.0 75.3 jit_solution(15597443674690780355)
XLA Ops:
  0.0 72.2 %shard_map.82 = f32[4096,128]{1,0:T(8,128)} custom-call(f32[3,128,512]{2,1,0:T(8,128)} %bitcast.10, s32[3,1,128]{2,1,0:T(1,128)} %bitcast.12, s32[3,1,128]{2,1,0:T(1,128)} %bitcast.13, f32[3,2,1024,128]{3,2,1,0:T(8,128)} %bitcast.8, f32[3,2,1024,128]{3,2,1,0:T(8,128)} %bitcast.9, f32[4,4]{1,0:T(4,128)} %bitcast.11, f32[4,4]{1,0:T(4,128)} %air_ref.1, ...), custom_call_target="tpu_custom_call" | custom-call | tf_op jit(solution)/shard_map/pallas_call | solution.py:576
  72.2 3.0 %copy.10 = f32[1,4,128,8,128]{4,3,2,1,0:T(8,128)} copy(f32[1,4,128,8,128]{4,3,2,1,0:T(8,128)} %bitcast.7) | data formatting | bytes 4194304
